TPU v7x, 256 devices: a whole 4x4x8 slice. The times are simulated.
256 devices in a mesh: dp: 256 (over z, y, x, core).
Axes of the slice: x: 4, y: 4, z: 8, core: 2. Of those that a mesh axis runs over, the one named last changes fastest.
Arguments:
- image_emb: bfloat16 [131072, 1152], P('dp'), may hold values from -0.19921875 to 0.19921875
- text_feat: bfloat16 [131072, 1152], P('dp'), may hold values from -6 to 6
- text_head: bfloat16 [1152, 1152], replicated, may hold values from -0.1875 to 0.1875
- pair_ids: int32 [131072], P('dp'), may hold values from 0 to 16383
- row_weight: bfloat16 [131072], P('dp'), as said below
Outputs:
- loss: float32 [1], replicated
- grad_image: bfloat16 [131072, 1152], P('dp')
- grad_text: bfloat16 [131072, 1152], P('dp')
- grad_head: bfloat16 [1152, 1152], replicated
Inputs may be any that keep to these rules, and one draw needn't show every extreme that they name: Every row_weight is positive.
All inputs are finite; a program needn't handle non-finite values.
Results may differ from a plain program's by a relative error of at most 0.012.
Values may be sent and summed in bfloat16 or wider, within the bound.
A program may use at most 128 MiB of HBM per device.

v0:
```python
import jax
import jax.numpy as jnp
from jax import lax
from jax.sharding import PartitionSpec as P

logit_scale = 10.0
logit_bias = -2.0
norm_eps = 1e-06


def swapped(block, axis, stride):
    count = lax.axis_size(axis)
    route = []
    for low in range(count):
        high = low | 1 << stride
        if high != low and high < count:
            route += [(low, high), (high, low)]
    return lax.ppermute(block, axis, route)


def normalize(values):
    length = jnp.sqrt(jnp.sum(values * values, axis=-1, keepdims=True) + norm_eps)
    return (values / length, length)


def signal(zi_rows, ids_rows, weight_rows, zt_cols, ids_cols):
    logit = (
        logit_scale
        * lax.dot_general(
            zi_rows, zt_cols, (((1,), (1,)), ((), ())), preferred_element_type=jnp.float32
        )
        + logit_bias
    )
    sign = jnp.where(ids_rows[:, None] == ids_cols[None, :], 1.0, -1.0).astype(jnp.float32)
    weight = weight_rows.astype(jnp.float32)[:, None]
    total = jnp.sum(weight * jax.nn.softplus(-sign * logit))
    dlog = (-sign * weight * jax.nn.sigmoid(-sign * logit)).astype(jnp.bfloat16)
    return (total, dlog)


def image_part(dlog, zt_cols):
    return logit_scale * jnp.dot(dlog, zt_cols, preferred_element_type=jnp.float32)


def text_part(dlog, zi_rows):
    product = lax.dot_general(
        dlog, zi_rows, (((0,), (0,)), ((), ())), preferred_element_type=jnp.float32
    )
    return (logit_scale * product).astype(jnp.bfloat16)


def shards(image_emb, text_feat, text_head, pair_ids, row_weight):
    rows = image_emb.shape[0]
    count = lax.axis_size("dp")
    u = jnp.dot(text_feat, text_head, preferred_element_type=jnp.float32)
    zt32, text_len = normalize(u)
    zt = zt32.astype(jnp.bfloat16)
    zi32, image_len = normalize(image_emb.astype(jnp.float32))
    zi = zi32.astype(jnp.bfloat16)
    loss_sum, dlog = signal(zi, pair_ids, row_weight, zt, pair_ids)
    dzi = image_part(dlog, zt)
    dzt = text_part(dlog, zi).astype(jnp.float32)
    for bit in [count.bit_length() - 2, 0]:
        far_text, far_ids = swapped((zt, pair_ids), "dp", bit)
        total, dlog = signal(zi, pair_ids, row_weight, far_text, far_ids)
        outgoing = text_part(dlog, zi)
        incoming = swapped(outgoing, "dp", bit)
        dzt = dzt + incoming.astype(jnp.float32)
        loss_sum = loss_sum + total
        dzi = dzi + image_part(dlog, far_text)
    grad_image = ((dzi - zi32 * jnp.sum(zi32 * dzi, axis=-1, keepdims=True)) / image_len).astype(
        jnp.bfloat16
    )
    du = ((dzt - zt32 * jnp.sum(zt32 * dzt, axis=-1, keepdims=True)) / text_len).astype(
        jnp.bfloat16
    )
    grad_text = lax.dot_general(
        du, text_head, (((1,), (1,)), ((), ())), preferred_element_type=jnp.float32
    ).astype(jnp.bfloat16)
    head_local = lax.dot_general(
        text_feat, du, (((0,), (0,)), ((), ())), preferred_element_type=jnp.float32
    )
    loss_all = lax.psum(loss_sum, "dp")
    head_out = lax.psum(head_local, "dp").astype(jnp.bfloat16)
    loss = (loss_all / (3.0 * rows * rows * count)).reshape(1)
    return (loss, grad_image, grad_text, head_out)


def solution(mesh):
    in_specs = (P("dp", None), P("dp", None), P(), P("dp"), P("dp"))
    out_specs = (P(), P("dp", None), P("dp", None), P())
    return jax.shard_map(shards, mesh=mesh, in_specs=in_specs, out_specs=out_specs, check_vma=False)
```

profile of v0, /device:TPU:1, one launch (start us, length us, event | category | flops | bytes accessed | tf_op | source)
XLA Modules:
  0.0 276.0 jit_solution(10600410227005088315)
XLA Ops:
  0.6 3.3 %collective-permute-start.2 = (s32[512]{0:T(512)}, s32[512]{0:T(512)S(1)}, u32[]{:S(2)}, u32[]{:S(2)}) collective-permute-start(s32[512]{0:T(512)} %param.8), channel_id=1, source_target_pairs={{0,1},{1,0},{2,3},{3,2},{4,5},{5,4},{6,7},{7,6},{8,9},{9,8},{10,11... | collective-permute-start | bytes 6152 | tf_op jit(solution)/shard_map/ppermute | solution.py:18
  4.0 5.2 %collective-permute-start = (s32[512]{0:T(512)}, s32[512]{0:T(512)S(1)}, u32[]{:S(2)}, u32[]{:S(2)}) collective-permute-start(s32[512]{0:T(512)} %param.8), channel_id=1, source_target_pairs={{0,128},{128,0},{1,129},{129,1},{2,130},{130,2},{3,131},{131,3},{4... | collective-permute-start | bytes 6152 | tf_op jit(solution)/shard_map/ppermute | solution.py:18
  9.2 3.2 %multiply_reduce_fusion.2 = (f32[512]{0:T(512)S(1)}, f32[512,1152]{1,0:T(8,128)S(1)}) fusion(bf16[512,1152]{1,0:T(8,128)(2,1)} %param.6, bf16[1152,1152]{1,0:T(8,128)(2,1)S(1)} %copy-done), kind=kOutput, calls=%fused_computation.23 | convolution fusion | flops 1360133632 | bytes 6195200 | tf_op jit(solution)/shard_map/dot_general | solution.py:55
  12.7 0.4 collective-permute-start.3
  13.2 1.3 collective-permute-start.1
  14.9 0.9 fusion.11
  15.8 1.1 fusion.19
  16.9 45.2 %collective-permute-done.1 = bf16[512,1152]{1,0:T(8,128)(2,1)S(1)} collective-permute-done((bf16[512,1152]{1,0:T(8,128)(2,1)S(1)}, bf16[512,1152]{1,0:T(8,128)(2,1)S(1)}, u32[]{:S(2)}, u32[]{:S(2)}) %collective-permute-start.1) | collective-permute-done | bytes 1179680 | tf_op jit(solution)/shard_map/ppermute | solution.py:18
  62.1 0.9 fusion.9
  63.1 2.2 fusion.3
  65.3 3.4 %fusion.17 = (f32[]{:T(128)}, f32[]{:T(128)}, f32[]{:T(128)}, f32[512,512]{1,0:T(8,128)S(1)}) fusion(f32[512]{0:T(512)S(1)} %convert_element_type.53, f32[512,512]{1,0:T(8,128)S(1)} %fusion.9, f32[512,512]{1,0:T(8,128)S(1)} %fusion.11, bf16[512,1152]{1,0:T(8,128)(2,1)S(1)} %collective-permute-done.3, f32[512]{0:T(512)S(1)} %add_sqrt_fusion.1, ...), kind=kOutput, calls=%fused_computation.39 | convolution fusion | flops 613613568 | bytes 5513228 | tf_op jit(solution)/shard_map/dot_general | solution.py:29
  68.7 2.2 fusion.4
  70.8 1.2 collective-permute-start.5
  72.0 1.1 convolution_add_fusion.1
  73.1 2.6 multiply_reduce_fusion.1
  77.7 3.7 %divide_convert_fusion.1 = bf16[512,1152]{1,0:T(8,128)(2,1)} fusion(f32[512,1152]{1,0:T(8,128)} %get-tuple-element.19, f32[512]{0:T(512)S(1)} %get-tuple-element.18, f32[512]{0:T(512)S(1)} %add_sqrt_fusion.1, bf16[512,1152]{1,0:T(8,128)(2,1)} %param.5), kind=kLoop, calls=%fused_computation.21 | loop fusion | flops 3538944 | bytes 4722688 | tf_op jit(solution)/shard_map/convert_element_type | solution.py:71
  81.3 15.2 %collective-permute-done.4 = bf16[512,1152]{1,0:T(8,128)(2,1)} collective-permute-done((bf16[512,1152]{1,0:T(8,128)(2,1)}, bf16[512,1152]{1,0:T(8,128)(2,1)}, u32[]{:S(2)}, u32[]{:S(2)}) %collective-permute-start.4) | collective-permute-done | bytes 1179680 | tf_op jit(solution)/shard_map/ppermute | solution.py:18
  96.6 3.3 %multiply_reduce_fusion = (f32[512]{0:T(512)S(1)}, f32[512,1152]{1,0:T(8,128)S(1)}) fusion(f32[512,1152]{1,0:T(8,128)S(1)} %copy-done.2, f32[512]{0:T(512)S(1)} %add_sqrt_fusion, bf16[512,1152]{1,0:T(8,128)(2,1)} %collective-permute-done.5, bf16[512,1152]{1,0:T(8,128)(2,1)} %collective-permute-done.4, f32[512]{0:T(512)S(1)} %add_sqrt_fusion.1, ...), kind=kOutput, calls=%fused_computation.19 | convolution fusion | flops 614006272 | bytes 9316352 | tf_op jit(solution)/shard_map/dot_general | solution.py:46
  99.8 0.4 divide_convert_fusion
  100.3 0.8 copy-done.5
  101.1 4.0 %convolution_bitcast_fusion = f32[1152,1152]{0,1:T(8,128)} fusion(bf16[512,1152]{1,0:T(8,128)(2,1)S(1)} %divide_convert_fusion, bf16[512,1152]{1,0:T(8,128)(2,1)S(1)} %copy-done.5), kind=kOutput, calls=%fused_computation | convolution fusion | flops 1358954496 | bytes 7667712 | tf_op jit(solution)/shard_map/dot_general | solution.py:80
  105.2 2.9 %convolution_convert_fusion = bf16[512,1152]{1,0:T(8,128)(2,1)} fusion(bf16[512,1152]{1,0:T(8,128)(2,1)S(1)} %divide_convert_fusion, bf16[1152,1152]{1,0:T(8,128)(2,1)S(1)} %copy-done), kind=kOutput, calls=%fused_computation.14 | convolution fusion | flops 1359544320 | bytes 5013504 | tf_op jit(solution)/shard_map/dot_general | solution.py:77
  108.1 160.9 %all-reduce.2 = (f32[]{:T(128)}, bf16[1152,1152]{0,1:T(8,128)(2,1)}) all-reduce(f32[]{:T(128)S(6)} %add.75, f32[1152,1152]{0,1:T(8,128)} %convolution_bitcast_fusion), channel_id=1, replica_groups=mesh['dp'=256] {'dp'}, use_global_device_ids=true, to_apply=%region_5.6 | all-reduce | flops 1327105 | bytes 7962632 | tf_op jit(solution)/shard_map/psum | solution.py:83
  269.0 5.2 %copy.9 = bf16[1152,1152]{1,0:T(8,128)(2,1)} copy(bf16[1152,1152]{0,1:T(8,128)(2,1)} %get-tuple-element.12) | data formatting | bytes 5308416
  (29 shorter events, 0.7 us)
Async XLA Ops:
  0.6 8.5 %copy-start = (bf16[1152,1152]{1,0:T(8,128)(2,1)S(1)}, bf16[1152,1152]{1,0:T(8,128)(2,1)}, u32[]{:S(2)}) copy-start(bf16[1152,1152]{1,0:T(8,128)(2,1)} %param.7) | copy-start | bytes 7962628
  0.6 64.6 %collective-permute-start.2 = (s32[512]{0:T(512)}, s32[512]{0:T(512)S(1)}, u32[]{:S(2)}, u32[]{:S(2)}) collective-permute-start(s32[512]{0:T(512)} %param.8), channel_id=1, source_target_pairs={{0,1},{1,0},{2,3},{3,2},{4,5},{5,4},{6,7},{7,6},{8,9},{9,8},{10,11... | collective-permute-start | bytes 6152 | tf_op jit(solution)/shard_map/ppermute | solution.py:18
  4.0 13.0 %collective-permute-start = (s32[512]{0:T(512)}, s32[512]{0:T(512)S(1)}, u32[]{:S(2)}, u32[]{:S(2)}) collective-permute-start(s32[512]{0:T(512)} %param.8), channel_id=1, source_target_pairs={{0,128},{128,0},{1,129},{129,1},{2,130},{130,2},{3,131},{131,3},{4... | collective-permute-start | bytes 6152 | tf_op jit(solution)/shard_map/ppermute | solution.py:18
  12.4 2.4 copy-start.1
  12.4 2.1 copy-start.3
  12.4 2.4 copy-start.6
  12.4 2.4 copy-start.7
  12.7 52.5 %collective-permute-start.3 = (bf16[512,1152]{1,0:T(8,128)(2,1)S(1)}, bf16[512,1152]{1,0:T(8,128)(2,1)S(1)}, u32[]{:S(2)}, u32[]{:S(2)}) collective-permute-start(bf16[512,1152]{1,0:T(8,128)(2,1)S(1)} %fusion.20), channel_id=1, source_target_pairs={{0,1},{1,0},{2,3},{3,2},{4,5},{5,4},{6,7},{7,6},{8,9},{9,8},{10,11... | collective-permute-start | bytes 3538952 | tf_op jit(solution)/shard_map/ppermute | solution.py:18
  13.2 48.9 %collective-permute-start.1 = (bf16[512,1152]{1,0:T(8,128)(2,1)S(1)}, bf16[512,1152]{1,0:T(8,128)(2,1)S(1)}, u32[]{:S(2)}, u32[]{:S(2)}) collective-permute-start(bf16[512,1152]{1,0:T(8,128)(2,1)S(1)} %fusion.20), channel_id=1, source_target_pairs={{0,128},{128,0},{1,129},{129,1},{2,130},{130,2},{3,131},{131,3},{4... | collective-permute-start | bytes 3538952 | tf_op jit(solution)/shard_map/ppermute | solution.py:18
  15.8 49.4 %copy-start.8 = (f32[512,512]{1,0:T(8,128)}, f32[512,512]{1,0:T(8,128)S(1)}, u32[]{:S(2)}) copy-start(f32[512,512]{1,0:T(8,128)S(1)} %fusion.11) | copy-start | bytes 3145732
  65.3 31.3 %collective-permute-start.4 = (bf16[512,1152]{1,0:T(8,128)(2,1)}, bf16[512,1152]{1,0:T(8,128)(2,1)}, u32[]{:S(2)}, u32[]{:S(2)}) collective-permute-start(bf16[512,1152]{1,0:T(8,128)(2,1)} %fusion.3), channel_id=1, source_target_pairs={{0,128},{128,0},{1,129},{129,1},{2,130},{130,2},{3,131},{131,3},{4... | collective-permute-start | bytes 3538952 | tf_op jit(solution)/shard_map/ppermute | solution.py:18
  70.8 25.7 %collective-permute-start.5 = (bf16[512,1152]{1,0:T(8,128)(2,1)}, bf16[512,1152]{1,0:T(8,128)(2,1)}, u32[]{:S(2)}, u32[]{:S(2)}) collective-permute-start(bf16[512,1152]{1,0:T(8,128)(2,1)} %fusion.4), channel_id=1, source_target_pairs={{0,1},{1,0},{2,3},{3,2},{4,5},{5,4},{6,7},{7,6},{8,9},{9,8},{10,11... | collective-permute-start | bytes 3538952 | tf_op jit(solution)/shard_map/ppermute | solution.py:18
  77.6 18.9 %copy-start.2 = (f32[512,1152]{1,0:T(8,128)S(1)}, f32[512,1152]{1,0:T(8,128)}, u32[]{:S(2)}) copy-start(f32[512,1152]{1,0:T(8,128)} %copy-done.1) | copy-start | bytes 7077892
  77.6 18.9 %copy-start.4 = (bf16[512,1152]{1,0:T(8,128)(2,1)S(1)}, bf16[512,1152]{1,0:T(8,128)(2,1)}, u32[]{:S(2)}) copy-start(bf16[512,1152]{1,0:T(8,128)(2,1)} %param.5) | copy-start | bytes 3538948
  77.7 18.9 %copy-start.9 = (f32[512,512]{1,0:T(8,128)S(1)}, f32[512,512]{1,0:T(8,128)}, u32[]{:S(2)}) copy-start(f32[512,512]{1,0:T(8,128)} %copy-done.8) | copy-start | bytes 3145732
  99.8 1.3 copy-start.5
where the time goes:
time: 277 us; the launch traced here: 276 us
  blocking collectives  161 us (58%)
  waiting for transfers between devices  60.4 us (22%)
  matrix products  27.8 us (10%)
  starting transfers between devices  11.5 us (4%)
  local copies, waits for them, and re-layouts  6.16 us (2%)
  other arithmetic  4.69 us (2%)
  between operations  4.54 us (2%)
    psum x1, blocking collectives, shards(): loss_all = lax.psum(loss_sum, 'dp')  161 us
    ppermute x6, waiting for transfers between devices, swapped(): return lax.ppermute(block, axis, route)  60.4 us
    ppermute x6, starting transfers between devices, swapped(): return lax.ppermute(block, axis, route)  11.5 us
    dot_general x3, matrix products, text_part(): lax.dot_general(dlog, zi_rows, (((0,), (0,)), ((), ())), preferred_elemen...  7.61 us
    unnamed x21, local copies, waits for them, and re-layouts  6.16 us
  transfers between devices with their start and end apart: 6, of which 2 were waited for; matrix products, arithmetic and copies ran while one was open for 8% of the time, Pallas kernels for 0%

commit v1 on v0

v1 whole, which is shorter than its diff:
```python
import functools

import jax
import jax.numpy as jnp
from jax import lax
from jax.experimental import pallas as pl
from jax.experimental.pallas import tpu as pltpu
from jax.sharding import PartitionSpec as P

MESH = pl.DeviceIdType.MESH
F32 = jnp.float32
BF16 = jnp.bfloat16

SCALE = 10.0
BIAS = -2.0
EPS = 1e-06

ROWS = 512
WIDTH = 1152
CHUNK = 128
CHUNKS = ROWS // CHUNK

UNITS = (WIDTH // 16) * (WIDTH // 128)
HALF = UNITS // 2
STREAM = HALF // 2
PIECE1 = 44
PIECE2 = 11
PIECE3 = 3


def dot_nt(a, b):
    return lax.dot_general(a, b, (((1,), (1,)), ((), ())), preferred_element_type=F32)


def dot_nn(a, b):
    return lax.dot_general(a, b, (((1,), (0,)), ((), ())), preferred_element_type=F32)


def dot_tn(a, b):
    return lax.dot_general(a, b, (((0,), (0,)), ((), ())), preferred_element_type=F32)


def rows_of(i, size=CHUNK):
    return pl.ds(pl.multiple_of(i * size, size), size)


def kernel(
    image_ref, text_ref, head_ref, ids_ref, weight_ref,
    loss_ref, gi_ref, gt_ref, gh_ref,
    image, text, head, zi, zi_inv, zt32, zt_inv, zt, zt_near, zt_far, text_far,
    ids_near, ids_far, dzt, dzi, part_near, got_near, part_far, got_far, du, du_far,
    dlog_own, dlog_near, dlog_far, loss_row, head_acc,
    units, got_a, half_b, got_b, sum_b, got_c, sum_c, got_d, gat_d, gat_c, gat_b, gat_a,
    loss_core, loss_x, loss_y, loss_z,
    load_sem, f_send, f_recv, id_send, id_recv, n_send, n_recv, np_send, np_recv, r_send, r_recv,
    a_send, a_recv, b_send, b_recv, c_send, c_recv, d_send, d_recv,
    e_send, e_recv, g_send, g_recv, h_send, h_recv, i_send, i_recv,
    l_send, l_recv, gate_sem,
):
    me = lax.axis_index("dp")
    core = me % 2
    x = (me // 2) % 4
    y = (me // 8) % 4
    z = me // 32

    def at(zz, yy, xx, cc):
        return ((zz * 4 + yy) * 4 + xx) * 2 + cc

    near = at(z, y, x, 1 - core)
    far = at((z + 4) % 8, y, x, core)

    def x_peer(d):
        return at(z, y, (x + d) % 4, core)

    def y_peer(d):
        return at(z, (y + d) % 4, x, core)

    def z_peer(d):
        return at((z + d) % 8, y, x, core)

    def remote(src, dst, send, recv, device):
        return pltpu.make_async_remote_copy(
            src_ref=src, dst_ref=dst, send_sem=send, recv_sem=recv,
            device_id=(device,), device_id_type=MESH,
        )

    loads = [
        pltpu.make_async_copy(head_ref, head, load_sem.at[0]),
        pltpu.make_async_copy(text_ref, text, load_sem.at[1]),
        pltpu.make_async_copy(image_ref, image, load_sem.at[2]),
    ]
    for load in loads:
        load.start()

    barrier = pltpu.get_barrier_semaphore()
    peers = [near] + [x_peer(d) for d in (1, 2, 3)] + [y_peer(d) for d in (1, 2, 3)] + [z_peer(d) for d in range(1, 8)]
    for peer in peers:
        pl.semaphore_signal(barrier, inc=1, device_id=(peer,), device_id_type=MESH)
    pl.semaphore_wait(barrier, len(peers))

    send_ids_far = remote(ids_ref, ids_far, id_send.at[0], id_recv.at[0], far)
    send_ids_near = remote(ids_ref, ids_near, id_send.at[1], id_recv.at[1], near)
    send_ids_far.start()
    send_ids_near.start()

    def forward(i):
        return remote(text_ref.at[rows_of(i)], text_far.at[rows_of(i)], f_send.at[i], f_recv.at[i], far)

    for i in range(CHUNKS):
        forward(i).start()

    loads[0].wait()
    loads[1].wait()

    def project(i, carry):
        rows = rows_of(i)
        u = dot_nn(text[rows, :], head[...])
        inv = 1.0 / jnp.sqrt(jnp.sum(u * u, axis=1, keepdims=True) + EPS)
        unit = u * inv
        zt32[rows, :] = unit
        zt_inv[rows, :] = inv
        zt[rows, :] = unit.astype(BF16)
        return carry

    lax.fori_loop(0, CHUNKS, project, 0)
    send_zt = remote(zt, zt_near, n_send, n_recv, near)
    send_zt.start()

    loads[2].wait()

    def image_norm(i, carry):
        rows = rows_of(i)
        v = image[rows, :].astype(F32)
        inv = 1.0 / jnp.sqrt(jnp.sum(v * v, axis=1, keepdims=True) + EPS)
        zi_inv[rows, :] = inv
        zi[rows, :] = (v * inv).astype(BF16)
        return carry

    lax.fori_loop(0, CHUNKS, image_norm, 0)

    own_ids = ids_ref[...]
    ids_image = jnp.concatenate([own_ids[i : i + 1, :] for i in range(CHUNKS)], axis=1)
    weight = weight_ref[...].astype(F32)
    loss_row[...] = jnp.zeros_like(loss_row)

    def tile(texts, ids_row):
        s = dot_nt(texts, zi[...])
        logit = SCALE * s + BIAS
        ids_col = jnp.transpose(jnp.broadcast_to(ids_row, (CHUNK, CHUNK)))[:, :1]
        same = ids_col == ids_image
        v = jnp.where(same, -logit, logit)
        e = jnp.exp(-jnp.abs(v))
        soft = jnp.maximum(v, 0.0) + jnp.log1p(e)
        loss_row[...] += jnp.sum(soft, axis=0, keepdims=True)
        sig = jnp.where(v >= 0.0, 1.0, e) / (1.0 + e)
        d = (jnp.where(same, -weight, weight) * sig).astype(BF16)
        part = (SCALE * dot_nn(d, zi[...])).astype(BF16)
        return d, part

    def own_tile(i, carry):
        rows = rows_of(i)
        d, part = tile(zt[rows, :], ids_ref[pl.ds(i, 1), :])
        dlog_own[rows, :] = d
        dzt[rows, :] = part.astype(F32)
        return carry

    lax.fori_loop(0, CHUNKS, own_tile, 0)

    send_ids_near.wait_recv()
    send_zt.wait_recv()

    def near_part(i):
        return remote(part_near.at[rows_of(i)], got_near.at[rows_of(i)], np_send.at[i], np_recv.at[i], near)

    def near_tile(i, carry):
        rows = rows_of(i)
        d, part = tile(zt_near[rows, :], ids_near[pl.ds(i, 1), :])
        dlog_near[rows, :] = d
        part_near[rows, :] = part
        near_part(i).start()
        return carry

    lax.fori_loop(0, CHUNKS, near_tile, 0)

    def image_grad(i, carry):
        cols = rows_of(i)
        dzi[cols, :] = dot_tn(dlog_own[:, cols], zt[...]) + dot_tn(dlog_near[:, cols], zt_near[...])
        return carry

    lax.fori_loop(0, CHUNKS, image_grad, 0)

    def own_du(i, carry):
        rows = rows_of(i)
        near_part(i).wait_recv()
        g = dzt[rows, :] + got_near[rows, :].astype(F32)
        dzt[rows, :] = g
        unit = zt32[rows, :]
        du[rows, :] = ((g - unit * jnp.sum(unit * g, axis=1, keepdims=True)) * zt_inv[rows, :]).astype(BF16)
        return carry

    lax.fori_loop(0, CHUNKS, own_du, 0)

    def head_own(i, carry):
        cols = rows_of(i)
        head_acc[cols, :] = dot_tn(text[:, cols], du[...])
        return carry

    lax.fori_loop(0, WIDTH // 128, head_own, 0)

    send_ids_far.wait_recv()

    def back(i):
        return remote(part_far.at[rows_of(i)], got_far.at[rows_of(i)], r_send.at[i], r_recv.at[i], far)

    def far_tile(i):
        rows = rows_of(i)
        u = dot_nn(text_far[rows, :], head[...])
        inv = 1.0 / jnp.sqrt(jnp.sum(u * u, axis=1, keepdims=True) + EPS)
        unit = u * inv
        texts = unit.astype(BF16)
        zt_far[rows, :] = texts
        d, part = tile(texts, ids_far[pl.ds(i, 1), :])
        dlog_far[rows, :] = d
        part_far[rows, :] = part
        g = part.astype(F32)
        du_far[rows, :] = ((g - unit * jnp.sum(unit * g, axis=1, keepdims=True)) * inv).astype(BF16)

    def far_step(i, carry):
        forward(i).wait_recv()

        @pl.when(i == CHUNKS - 1)
        def _():
            pl.semaphore_signal(gate_sem, inc=1, device_id=(z_peer(6),), device_id_type=MESH)
            pl.semaphore_wait(gate_sem, 1)
            for j in range(CHUNKS - 1):
                back(j).start()

        far_tile(i)
        return carry

    lax.fori_loop(0, CHUNKS, far_step, 0)
    back(CHUNKS - 1).start()

    def head_all(i, carry):
        cols = rows_of(i)
        total = head_acc[cols, :] + dot_tn(text_far[:, cols], du_far[...])
        out = total.astype(BF16)
        for r in range(8):
            for c in range(9):
                units[i * 72 + (r * 9 + c)] = out[16 * r : 16 * r + 16, 128 * c : 128 * c + 128]
        return carry

    lax.fori_loop(0, WIDTH // 128, head_all, 0)
    loss_core[core] = jnp.broadcast_to(jnp.sum(weight * loss_row[...]).reshape(1, 1), (8, 128))

    copy_a = remote(units.at[pl.ds((1 - core) * HALF, HALF)], got_a, a_send, a_recv, near)
    copy_a.start()
    loss_a = remote(loss_core.at[core], loss_core.at[core], l_send.at[0], l_recv.at[0], near)
    loss_a.start()

    def finish_image(i, carry):
        rows = rows_of(i)
        g = SCALE * (dzi[rows, :] + dot_tn(dlog_far[:, rows], zt_far[...]))
        inv = zi_inv[rows, :]
        unit = image[rows, :].astype(F32) * inv
        gi_ref[rows, :] = ((g - unit * jnp.sum(unit * g, axis=1, keepdims=True)) * inv).astype(BF16)
        return carry

    def finish_text(i):
        back(i).wait_recv()
        rows = rows_of(i)
        g = dzt[rows, :] + got_far[rows, :].astype(F32)
        unit = zt32[rows, :]
        d = ((g - unit * jnp.sum(unit * g, axis=1, keepdims=True)) * zt_inv[rows, :]).astype(BF16)
        gt_ref[rows, :] = dot_nt(d, head[...]).astype(BF16)

    copy_a.wait_recv()
    loss_a.wait_recv()
    loss_x[x] = loss_core[0] + loss_core[1]

    def add_a(i, carry):
        own = units[pl.ds(core * HALF + i * 12, 12)].astype(F32)
        half_b[pl.ds(i * 12, 12)] = (own + got_a[pl.ds(i * 12, 12)].astype(F32)).astype(BF16)
        return carry

    lax.fori_loop(0, HALF // 12, add_a, 0)
    half_b[pl.ds(HALF, 16)] = jnp.zeros((16, 16, 128), BF16)

    first = [(x_peer, x), (y_peer, y)]
    second = [(y_peer, y), (x_peer, x)]
    copies_b = []
    for s in range(2):
        peer, at_s = first[s]
        for d in (1, 2, 3):
            to = (at_s + d) % 4
            k = 3 * s + d - 1
            copies_b.append(remote(half_b.at[pl.ds(STREAM * s + PIECE1 * to, PIECE1)], got_b.at[k], b_send.at[k], b_recv.at[k], peer(d)))
    loss_b = [remote(loss_x.at[x], loss_x.at[x], l_send.at[d], l_recv.at[d], x_peer(d)) for d in (1, 2, 3)]
    for copy in copies_b + loss_b:
        copy.start()

    lax.fori_loop(0, CHUNKS, finish_image, 0)

    for copy in copies_b + loss_b:
        copy.wait_recv()
    loss_y[y] = (loss_x[0] + loss_x[1]) + (loss_x[2] + loss_x[3])
    for s in range(2):
        base = STREAM * s + PIECE1 * first[s][1]

        def add_b(i, carry, s=s, base=base):
            total = half_b[pl.ds(base + i * 11, 11)].astype(F32)
            for k in range(3 * s, 3 * s + 3):
                total = total + got_b[k, pl.ds(i * 11, 11)].astype(F32)
            sum_b[s, pl.ds(i * 11, 11)] = total.astype(BF16)
            return carry

        lax.fori_loop(0, 4, add_b, 0)

    copies_c = []
    for s in range(2):
        peer, at_s = second[s]
        for d in (1, 2, 3):
            to = (at_s + d) % 4
            k = 3 * s + d - 1
            copies_c.append(remote(sum_b.at[s, pl.ds(PIECE2 * to, PIECE2)], got_c.at[k], c_send.at[k], c_recv.at[k], peer(d)))
    loss_c = [remote(loss_y.at[y], loss_y.at[y], l_send.at[3 + d], l_recv.at[3 + d], y_peer(d)) for d in (1, 2, 3)]
    for copy in copies_c + loss_c:
        copy.start()
    for copy in copies_c + loss_c:
        copy.wait_recv()
    loss_z[z] = (loss_y[0] + loss_y[1]) + (loss_y[2] + loss_y[3])
    for s in range(2):
        total = sum_b[s, pl.ds(PIECE2 * second[s][1], PIECE2)].astype(F32)
        for k in range(3 * s, 3 * s + 3):
            total = total + got_c[k].astype(F32)
        sum_c[pl.ds(PIECE2 * s, PIECE2)] = total.astype(BF16)
    sum_c[pl.ds(2 * PIECE2, 2)] = jnp.zeros((2, 16, 128), BF16)

    copies_d = []
    for d in range(1, 8):
        to = (z + d) % 8
        copies_d.append(remote(sum_c.at[pl.ds(PIECE3 * to, PIECE3)], got_d.at[d - 1], d_send.at[d - 1], d_recv.at[d - 1], z_peer(d)))
    loss_d = [remote(loss_z.at[z], loss_z.at[z], l_send.at[6 + d], l_recv.at[6 + d], z_peer(d)) for d in range(1, 8)]
    for copy in copies_d + loss_d:
        copy.start()
    for copy in copies_d + loss_d:
        copy.wait_recv()
    total = sum_c[pl.ds(PIECE3 * z, PIECE3)].astype(F32)
    for k in range(7):
        total = total + got_d[k].astype(F32)
    gat_d[pl.ds(PIECE3 * z, PIECE3)] = total.astype(BF16)
    sums = [loss_z[k] for k in range(8)]
    loss_all = ((sums[0] + sums[1]) + (sums[2] + sums[3])) + ((sums[4] + sums[5]) + (sums[6] + sums[7]))
    loss_ref[0] = jnp.max(loss_all) / (3.0 * ROWS * ROWS * 256)

    mine = gat_d.at[pl.ds(PIECE3 * z, PIECE3)]
    copies_e = [remote(mine, mine, e_send.at[d - 1], e_recv.at[d - 1], z_peer(d)) for d in range(1, 8)]
    for copy in copies_e:
        copy.start()
    finish_text(0)
    for copy in copies_e:
        copy.wait_recv()

    copies_g = []
    for s in range(2):
        peer, at_s = second[s]
        src = gat_d.at[pl.ds(PIECE2 * s, PIECE2)]
        dst = gat_c.at[s, pl.ds(PIECE2 * at_s, PIECE2)]
        for d in (1, 2, 3):
            k = 3 * s + d - 1
            copies_g.append(remote(src, dst, g_send.at[k], g_recv.at[k], peer(d)))
    for copy in copies_g:
        copy.start()
    for s in range(2):
        gat_c[s, pl.ds(PIECE2 * second[s][1], PIECE2)] = gat_d[pl.ds(PIECE2 * s, PIECE2)]
    for copy in copies_g:
        copy.wait_recv()

    copies_h = []
    for s in range(2):
        peer, at_s = first[s]
        dst = gat_b.at[s, pl.ds(PIECE1 * at_s, PIECE1)]
        for d in (1, 2, 3):
            k = 3 * s + d - 1
            copies_h.append(remote(gat_c.at[s], dst, h_send.at[k], h_recv.at[k], peer(d)))
    for copy in copies_h:
        copy.start()
    for s in range(2):
        gat_b[s, pl.ds(PIECE1 * first[s][1], PIECE1)] = gat_c[s]
    finish_text(1)
    for copy in copies_h:
        copy.wait_recv()

    copy_i = remote(gat_b, gat_a, i_send, i_recv, near)
    copy_i.start()

    def write_head(src, which):
        for s in range(2):

            def body(r, carry, s=s):
                row = pl.ds(pl.multiple_of(which * (HALF // 9 * 16) + s * (STREAM // 9 * 16) + r * 16, 16), 16)
                for c in range(9):
                    gh_ref[row, 128 * c : 128 * c + 128] = src[s, r * 9 + c]
                return carry

            lax.fori_loop(0, STREAM // 9, body, 0)

    write_head(gat_b, core)
    copy_i.wait_recv()
    write_head(gat_a, 1 - core)

    for i in range(2, CHUNKS):
        finish_text(i)

    send_ids_far.wait_send()
    send_ids_near.wait_send()
    for i in range(CHUNKS):
        forward(i).wait_send()
        near_part(i).wait_send()
        back(i).wait_send()
    for copy in [send_zt, copy_a, loss_a, copy_i] + copies_b + loss_b + copies_c + loss_c + copies_d + loss_d + copies_e + copies_g + copies_h:
        copy.wait_send()


def shards(image_emb, text_feat, text_head, pair_ids, row_weight):
    anywhere = pl.BlockSpec(memory_space=pl.ANY)
    vmem = pl.BlockSpec(memory_space=pltpu.VMEM)
    block = (ROWS, WIDTH)
    dma = pltpu.SemaphoreType.DMA
    unit = (16, 128)
    scratch = [
        pltpu.VMEM(block, BF16),
        pltpu.VMEM(block, BF16),
        pltpu.VMEM((WIDTH, WIDTH), BF16),
        pltpu.VMEM(block, BF16),
        pltpu.VMEM((ROWS, 1), F32),
        pltpu.VMEM(block, F32),
        pltpu.VMEM((ROWS, 1), F32),
        pltpu.VMEM(block, BF16),
        pltpu.VMEM(block, BF16),
        pltpu.VMEM(block, BF16),
        pltpu.VMEM(block, BF16),
        pltpu.VMEM((4, 128), jnp.int32),
        pltpu.VMEM((4, 128), jnp.int32),
        pltpu.VMEM(block, F32),
        pltpu.VMEM(block, F32),
        pltpu.VMEM(block, BF16),
        pltpu.VMEM(block, BF16),
        pltpu.VMEM(block, BF16),
        pltpu.VMEM(block, BF16),
        pltpu.VMEM(block, BF16),
        pltpu.VMEM(block, BF16),
        pltpu.VMEM((ROWS, ROWS), BF16),
        pltpu.VMEM((ROWS, ROWS), BF16),
        pltpu.VMEM((ROWS, ROWS), BF16),
        pltpu.VMEM((1, ROWS), F32),
        pltpu.VMEM((WIDTH, WIDTH), F32),
        pltpu.VMEM((UNITS,) + unit, BF16),
        pltpu.VMEM((HALF,) + unit, BF16),
        pltpu.VMEM((HALF + 16,) + unit, BF16),
        pltpu.VMEM((6, PIECE1) + unit, BF16),
        pltpu.VMEM((2, PIECE1) + unit, BF16),
        pltpu.VMEM((6, PIECE2) + unit, BF16),
        pltpu.VMEM((8 * PIECE3,) + unit, BF16),
        pltpu.VMEM((7, PIECE3) + unit, BF16),
        pltpu.VMEM((8 * PIECE3,) + unit, BF16),
        pltpu.VMEM((2, PIECE1) + unit, BF16),
        pltpu.VMEM((2, 4 * PIECE1) + unit, BF16),
        pltpu.VMEM((2, 4 * PIECE1) + unit, BF16),
        pltpu.VMEM((2, 8, 128), F32),
        pltpu.VMEM((4, 8, 128), F32),
        pltpu.VMEM((4, 8, 128), F32),
        pltpu.VMEM((8, 8, 128), F32),
        dma((3,)),
        dma((CHUNKS,)), dma((CHUNKS,)),
        dma((2,)), dma((2,)),
        dma, dma,
        dma((CHUNKS,)), dma((CHUNKS,)),
        dma((CHUNKS,)), dma((CHUNKS,)),
        dma, dma,
        dma((6,)), dma((6,)),
        dma((6,)), dma((6,)),
        dma((7,)), dma((7,)),
        dma((7,)), dma((7,)),
        dma((6,)), dma((6,)),
        dma((6,)), dma((6,)),
        dma, dma,
        dma((14,)), dma((14,)),
        pltpu.SemaphoreType.REGULAR,
    ]
    return pl.pallas_call(
        kernel,
        out_shape=(
            jax.ShapeDtypeStruct((1,), F32),
            jax.ShapeDtypeStruct(block, BF16),
            jax.ShapeDtypeStruct(block, BF16),
            jax.ShapeDtypeStruct((WIDTH, WIDTH), BF16),
        ),
        in_specs=[anywhere, anywhere, anywhere, vmem, vmem],
        out_specs=(pl.BlockSpec(memory_space=pltpu.SMEM), vmem, vmem, vmem),
        scratch_shapes=scratch,
        compiler_params=pltpu.CompilerParams(
            collective_id=0, has_side_effects=True, vmem_limit_bytes=58 * 1024 * 1024
        ),
        name="contrast",
    )(image_emb, text_feat, text_head, pair_ids.reshape(4, 128), row_weight.reshape(1, ROWS))


def solution(mesh):
    in_specs = (P("dp", None), P("dp", None), P(), P("dp"), P("dp"))
    out_specs = (P(), P("dp", None), P("dp", None), P())
    return jax.shard_map(shards, mesh=mesh, in_specs=in_specs, out_specs=out_specs, check_vma=False)
```

time: 277 us -> 160 us (0.58)
  blocking collectives: 161 us -> 0 us
  Pallas kernels: 0 us -> 150 us
  waiting for transfers between devices: 60.4 us -> 0 us
  matrix products: 27.8 us -> 0 us
  starting transfers between devices: 11.5 us -> 0 us
  other arithmetic: 4.69 us -> 0 us
    psum x1 -> x0, blocking collectives: 161 us -> none  [shards(): loss_all = lax.psum(loss_sum, 'dp')]
    pallas_call x0 -> x1, Pallas kernels: none -> 150 us  [shards(): pl.pallas_call(kernel, out_shape=(jax.ShapeDtypeStruct((1,), F32), jax.Sh...]
    ppermute x6 -> x0, waiting for transfers between devices: 60.4 us -> none  [swapped(): return lax.ppermute(block, axis, route)]
    dot_general x12 -> x0, matrix products: 27.8 us -> none  [the longest x3 7.61 us: text_part(): lax.dot_general(dlog, zi_rows, (((0,), (0,)), ((), ())), preferred_elemen...]
    ppermute x6 -> x0, starting transfers between devices: 11.5 us -> none  [swapped(): return lax.ppermute(block, axis, route)]
    convert_element_type x4 -> x0, other arithmetic: 4.37 us -> none  [the longest x1 3.66 us: shards(): ((dzi - zi32 * jnp.sum(zi32 * dzi, axis=-1, keepdims=True)) / image_len)....]
    unnamed x21 -> x5, local copies, waits for them, and re-layouts: 6.16 us -> 6.4 us
  transfers between devices with their start and end apart: 6 -> 0, of which waited for: 2 -> 0; matrix products, arithmetic and copies ran while one was open for 8% -> 0% of each run, Pallas kernels for 0% -> 0%
where the time goes in v1:
time: 160 us
  Pallas kernels  150 us (94%)
  local copies, waits for them, and re-layouts  7.66 us (5%)
  between operations  2.46 us (2%)
    pallas_call x1, Pallas kernels, shards(): pl.pallas_call(kernel, out_shape=(jax.ShapeDtypeStruct((1,), F32), jax.Sh...  150 us
    unnamed x5, local copies, waits for them, and re-layouts  6.4 us

profile of v1, /device:TPU:1, one launch (start us, length us, event | category | flops | bytes accessed | tf_op | source)
XLA Modules:
  0.0 159.7 jit_solution(8743942993875580591)
XLA Ops:
  0.6 1.3 reshape.15.weight_ref
  1.9 149.6 %contrast.1 = (f32[1]{0:T(128)}, bf16[512,1152]{1,0:T(8,128)(2,1)}, bf16[512,1152]{1,0:T(8,128)(2,1)}, bf16[1152,1152]{1,0:T(8,128)(2,1)}) custom-call(bf16[512,1152]{1,0:T(8,128)(2,1)} %image_ref.1, bf16[512,1152]{1,0:T(8,128)(2,1)} %text_ref.1, bf16[1152,1152]{1,0:T(8,128)(2,1)} %head_ref.1, s32[4,128]{1,0:T(4,128)} %bitcast.1, ...), custom_call_target="tpu_custom_call" | custom-call | tf_op jit(solution)/shard_map/contrast/pallas_call | solution.py:491
  152.2 0.0 copy-start
  152.2 2.5 %copy.14 = bf16[512,1152]{1,0:T(8,128)(2,1)} copy(bf16[512,1152]{1,0:T(8,128)(2,1)} %get-tuple-element.9) | data formatting | bytes 2359296
  154.7 2.4 %copy.15 = bf16[512,1152]{1,0:T(8,128)(2,1)} copy(bf16[512,1152]{1,0:T(8,128)(2,1)} %get-tuple-element.10) | data formatting | bytes 2359296
  157.1 0.0 copy-done
  157.1 1.5 copy.16
Async XLA Ops:
  152.2 4.9 %copy-start = (bf16[1152,1152]{1,0:T(8,128)(2,1)S(1)}, bf16[1152,1152]{1,0:T(8,128)(2,1)}, u32[]{:S(2)}) copy-start(bf16[1152,1152]{1,0:T(8,128)(2,1)} %get-tuple-element.11) | copy-start | bytes 7962628

commit v2 on v1

--- a/solution.py
+++ b/solution.py
@@ -19,6 +19,11 @@
 WIDTH = 1152
 CHUNK = 128
 CHUNKS = ROWS // CHUNK
+BACK = 64
+BACKS = ROWS // BACK
+BACK_1 = 4
+BACK_2 = 5
+PIECES = 4
 
 UNITS = (WIDTH // 16) * (WIDTH // 128)
 HALF = UNITS // 2
@@ -51,11 +56,11 @@
     ids_near, ids_far, dzt, dzi, part_near, got_near, part_far, got_far, du, du_far,
     dlog_own, dlog_near, dlog_far, loss_row, head_acc,
     units, got_a, half_b, got_b, sum_b, got_c, sum_c, got_d, gat_d, gat_c, gat_b, gat_a,
-    loss_core, loss_x, loss_y, loss_z,
+    loss_core, loss_x, loss_y, loss_z, gi, gt, gh,
     load_sem, f_send, f_recv, id_send, id_recv, n_send, n_recv, np_send, np_recv, r_send, r_recv,
     a_send, a_recv, b_send, b_recv, c_send, c_recv, d_send, d_recv,
     e_send, e_recv, g_send, g_recv, h_send, h_recv, i_send, i_recv,
-    l_send, l_recv, gate_sem,
+    l_send, l_recv, gate_sem, out_sem,
 ):
     me = lax.axis_index("dp")
     core = me % 2
@@ -140,7 +145,7 @@
 
     own_ids = ids_ref[...]
     ids_image = jnp.concatenate([own_ids[i : i + 1, :] for i in range(CHUNKS)], axis=1)
-    weight = weight_ref[...].astype(F32)
+    weight = weight_ref[...].astype(F32).reshape(1, ROWS)
     loss_row[...] = jnp.zeros_like(loss_row)
 
     def tile(texts, ids_row):
@@ -210,7 +215,12 @@
     send_ids_far.wait_recv()
 
     def back(i):
-        return remote(part_far.at[rows_of(i)], got_far.at[rows_of(i)], r_send.at[i], r_recv.at[i], far)
+        rows = rows_of(i, BACK)
+        return remote(part_far.at[rows], got_far.at[rows], r_send.at[i], r_recv.at[i], far)
+
+    def send_back(first, last):
+        for j in range(first, last):
+            back(j).start()
 
     def far_tile(i):
         rows = rows_of(i)
@@ -232,16 +242,15 @@
         def _():
             pl.semaphore_signal(gate_sem, inc=1, device_id=(z_peer(6),), device_id_type=MESH)
             pl.semaphore_wait(gate_sem, 1)
-            for j in range(CHUNKS - 1):
-                back(j).start()
+            send_back(0, BACK_1)
 
         far_tile(i)
         return carry
 
     lax.fori_loop(0, CHUNKS, far_step, 0)
-    back(CHUNKS - 1).start()
 
     def head_all(i, carry):
+        i = (i + 4 * (1 - core)) % 9
         cols = rows_of(i)
         total = head_acc[cols, :] + dot_tn(text_far[:, cols], du_far[...])
         out = total.astype(BF16)
@@ -250,11 +259,12 @@
                 units[i * 72 + (r * 9 + c)] = out[16 * r : 16 * r + 16, 128 * c : 128 * c + 128]
         return carry
 
-    lax.fori_loop(0, WIDTH // 128, head_all, 0)
-    loss_core[core] = jnp.broadcast_to(jnp.sum(weight * loss_row[...]).reshape(1, 1), (8, 128))
-
+    lax.fori_loop(0, 5, head_all, 0)
     copy_a = remote(units.at[pl.ds((1 - core) * HALF, HALF)], got_a, a_send, a_recv, near)
     copy_a.start()
+    lax.fori_loop(5, 9, head_all, 0)
+    loss_core[core] = jnp.broadcast_to(jnp.sum(weight * loss_row[...]).reshape(1, 1), (8, 128))
+
     loss_a = remote(loss_core.at[core], loss_core.at[core], l_send.at[0], l_recv.at[0], near)
     loss_a.start()
 
@@ -263,16 +273,21 @@
         g = SCALE * (dzi[rows, :] + dot_tn(dlog_far[:, rows], zt_far[...]))
         inv = zi_inv[rows, :]
         unit = image[rows, :].astype(F32) * inv
-        gi_ref[rows, :] = ((g - unit * jnp.sum(unit * g, axis=1, keepdims=True)) * inv).astype(BF16)
-        return carry
+        gi[rows, :] = ((g - unit * jnp.sum(unit * g, axis=1, keepdims=True)) * inv).astype(BF16)
+        return carry
+
+    def put_text(i):
+        return pltpu.make_async_copy(gt.at[rows_of(i)], gt_ref.at[rows_of(i)], out_sem.at[i])
 
     def finish_text(i):
-        back(i).wait_recv()
+        for j in range(i * CHUNK // BACK, (i + 1) * CHUNK // BACK):
+            back(j).wait_recv()
         rows = rows_of(i)
         g = dzt[rows, :] + got_far[rows, :].astype(F32)
         unit = zt32[rows, :]
         d = ((g - unit * jnp.sum(unit * g, axis=1, keepdims=True)) * zt_inv[rows, :]).astype(BF16)
-        gt_ref[rows, :] = dot_nt(d, head[...]).astype(BF16)
+        gt[rows, :] = dot_nt(d, head[...]).astype(BF16)
+        put_text(i).start()
 
     copy_a.wait_recv()
     loss_a.wait_recv()
@@ -300,6 +315,8 @@
         copy.start()
 
     lax.fori_loop(0, CHUNKS, finish_image, 0)
+    put_image = pltpu.make_async_copy(gi, gi_ref, out_sem.at[CHUNKS])
+    put_image.start()
 
     for copy in copies_b + loss_b:
         copy.wait_recv()
@@ -343,6 +360,7 @@
     loss_d = [remote(loss_z.at[z], loss_z.at[z], l_send.at[6 + d], l_recv.at[6 + d], z_peer(d)) for d in range(1, 8)]
     for copy in copies_d + loss_d:
         copy.start()
+    send_back(BACK_1, BACK_2)
     for copy in copies_d + loss_d:
         copy.wait_recv()
     total = sum_c[pl.ds(PIECE3 * z, PIECE3)].astype(F32)
@@ -358,8 +376,10 @@
     for copy in copies_e:
         copy.start()
     finish_text(0)
+    finish_text(1)
     for copy in copies_e:
         copy.wait_recv()
+    send_back(BACK_2, BACKS)
 
     copies_g = []
     for s in range(2):
@@ -387,7 +407,6 @@
         copy.start()
     for s in range(2):
         gat_b[s, pl.ds(PIECE1 * first[s][1], PIECE1)] = gat_c[s]
-    finish_text(1)
     for copy in copies_h:
         copy.wait_recv()
 
@@ -400,14 +419,20 @@
             def body(r, carry, s=s):
                 row = pl.ds(pl.multiple_of(which * (HALF // 9 * 16) + s * (STREAM // 9 * 16) + r * 16, 16), 16)
                 for c in range(9):
-                    gh_ref[row, 128 * c : 128 * c + 128] = src[s, r * 9 + c]
+                    gh[row, 128 * c : 128 * c + 128] = src[s, r * 9 + c]
                 return carry
 
             lax.fori_loop(0, STREAM // 9, body, 0)
 
+    def put_head(which, k):
+        rows = rows_of(which, WIDTH // 2)
+        return pltpu.make_async_copy(gh.at[rows], gh_ref.at[rows], out_sem.at[CHUNKS + 1 + k])
+
     write_head(gat_b, core)
+    put_head(core, 0).start()
     copy_i.wait_recv()
     write_head(gat_a, 1 - core)
+    put_head(1 - core, 1).start()
 
     for i in range(2, CHUNKS):
         finish_text(i)
@@ -417,9 +442,33 @@
     for i in range(CHUNKS):
         forward(i).wait_send()
         near_part(i).wait_send()
+    for i in range(BACKS):
         back(i).wait_send()
     for copy in [send_zt, copy_a, loss_a, copy_i] + copies_b + loss_b + copies_c + loss_c + copies_d + loss_d + copies_e + copies_g + copies_h:
         copy.wait_send()
+    for i in range(CHUNKS):
+        put_text(i).wait()
+    put_image.wait()
+    put_head(core, 0).wait()
+    put_head(1 - core, 1).wait()
+
+
+def move(a_ref, b_ref, c_ref, a_out, b_out, c_out, a_buf, b_buf, c_buf, sem, sem2):
+    ins = []
+    outs = []
+    for k, (src, buf, dst) in enumerate([(a_ref, a_buf, a_out), (b_ref, b_buf, b_out), (c_ref, c_buf, c_out)]):
+        size = src.shape[0] // PIECES
+        for i in range(PIECES):
+            rows = pl.ds(i * size, size)
+            ins.append(pltpu.make_async_copy(src.at[rows], buf.at[rows], sem.at[k * PIECES + i]))
+            outs.append(pltpu.make_async_copy(buf.at[rows], dst.at[rows], sem2.at[k * PIECES + i]))
+    for copy in ins:
+        copy.start()
+    for copy, out in zip(ins, outs):
+        copy.wait()
+        out.start()
+    for copy in outs:
+        copy.wait()
 
 
 def shards(image_emb, text_feat, text_head, pair_ids, row_weight):
@@ -471,12 +520,15 @@
         pltpu.VMEM((4, 8, 128), F32),
         pltpu.VMEM((4, 8, 128), F32),
         pltpu.VMEM((8, 8, 128), F32),
+        pltpu.VMEM(block, BF16),
+        pltpu.VMEM(block, BF16),
+        pltpu.VMEM((WIDTH, WIDTH), BF16),
         dma((3,)),
         dma((CHUNKS,)), dma((CHUNKS,)),
         dma((2,)), dma((2,)),
         dma, dma,
         dma((CHUNKS,)), dma((CHUNKS,)),
-        dma((CHUNKS,)), dma((CHUNKS,)),
+        dma((BACKS,)), dma((BACKS,)),
         dma, dma,
         dma((6,)), dma((6,)),
         dma((6,)), dma((6,)),
@@ -487,8 +539,9 @@
         dma, dma,
         dma((14,)), dma((14,)),
         pltpu.SemaphoreType.REGULAR,
+        dma((CHUNKS + 3,)),
     ]
-    return pl.pallas_call(
+    loss, *grads = pl.pallas_call(
         kernel,
         out_shape=(
             jax.ShapeDtypeStruct((1,), F32),
@@ -497,13 +550,22 @@
             jax.ShapeDtypeStruct((WIDTH, WIDTH), BF16),
         ),
         in_specs=[anywhere, anywhere, anywhere, vmem, vmem],
-        out_specs=(pl.BlockSpec(memory_space=pltpu.SMEM), vmem, vmem, vmem),
+        out_specs=(pl.BlockSpec(memory_space=pltpu.SMEM), anywhere, anywhere, anywhere),
         scratch_shapes=scratch,
         compiler_params=pltpu.CompilerParams(
             collective_id=0, has_side_effects=True, vmem_limit_bytes=58 * 1024 * 1024
         ),
         name="contrast",
-    )(image_emb, text_feat, text_head, pair_ids.reshape(4, 128), row_weight.reshape(1, ROWS))
+    )(image_emb, text_feat, text_head, pair_ids.reshape(4, 128), row_weight)
+    moved = pl.pallas_call(
+        move,
+        out_shape=tuple(jax.ShapeDtypeStruct(g.shape, BF16) for g in grads),
+        in_specs=[anywhere] * 3,
+        out_specs=(anywhere,) * 3,
+        scratch_shapes=[pltpu.VMEM(g.shape, BF16) for g in grads] + [dma((3 * PIECES,)), dma((3 * PIECES,))],
+        name="move",
+    )(*grads)
+    return (loss, *moved)
 
 
 def solution(mesh):

time: 160 us -> 139 us (0.87)
  Pallas kernels: 150 us -> 135 us
  local copies, waits for them, and re-layouts: 7.66 us -> 0 us
    pallas_call x1, Pallas kernels: 150 us -> 130 us  [shards(): pl.pallas_call(kernel, out_shape=(jax.ShapeDtypeStruct((1,), F32), jax.Sh...]
    unnamed x5 -> x0, local copies, waits for them, and re-layouts: 6.4 us -> none
    pallas_call x0 -> x1, Pallas kernels: none -> 4.78 us  [shards(): pl.pallas_call(move, out_shape=tuple((jax.ShapeDtypeStruct(g.shape, BF16)...]
where the time goes in v2:
time: 139 us; the launch traced here: 138 us
  Pallas kernels  135 us (97%)
  between operations  2.46 us (2%)
    pallas_call x1, Pallas kernels, shards(): pl.pallas_call(kernel, out_shape=(jax.ShapeDtypeStruct((1,), F32), jax.Sh...  130 us
    pallas_call x1, Pallas kernels, shards(): pl.pallas_call(move, out_shape=tuple((jax.ShapeDtypeStruct(g.shape, BF16)...  4.78 us

profile of v2, /device:TPU:1, one launch (start us, length us, event | category | flops | bytes accessed | tf_op | source)
XLA Modules:
  0.0 137.5 jit_solution(12865478687796446653)
XLA Ops:
  0.6 130.3 %contrast.1 = (f32[1]{0:T(128)}, bf16[512,1152]{1,0:T(8,128)(2,1)}, bf16[512,1152]{1,0:T(8,128)(2,1)}, bf16[1152,1152]{1,0:T(8,128)(2,1)}) custom-call(bf16[512,1152]{1,0:T(8,128)(2,1)} %image_ref.1, bf16[512,1152]{1,0:T(8,128)(2,1)} %text_ref.1, bf16[1152,1152]{1,0:T(8,128)(2,1)} %head_ref.1, s32[4,128]{1,0:T(4,128)} %bitcast.1, bf16[512]{0:T(512)(128)(2,1)} %weight_ref.1), custom_call_target="tpu_custom_call" | custom-call | tf_op jit(solution)/shard_map/contrast/pallas_call | solution.py:544
  130.9 4.8 %move.1 = (bf16[512,1152]{1,0:T(8,128)(2,1)}, bf16[512,1152]{1,0:T(8,128)(2,1)}, bf16[1152,1152]{1,0:T(8,128)(2,1)}) custom-call(bf16[512,1152]{1,0:T(8,128)(2,1)} %get-tuple-element.12.a_ref, bf16[512,1152]{1,0:T(8,128)(2,1)} %get-tuple-element.13.b_ref, bf16[1152,1152]{1,0:T(8,128)(2,1)} %get-tuple-element.14.c_ref), custom_call_target="tpu_custom_call" | custom-call | tf_op jit(solution)/shard_map/move/pallas_call | solution.py:560

commit v3 on v1

--- a/solution.py
+++ b/solution.py
@@ -19,6 +19,10 @@
 WIDTH = 1152
 CHUNK = 128
 CHUNKS = ROWS // CHUNK
+BACK = 64
+BACKS = ROWS // BACK
+BACK_1 = 4
+BACK_2 = 5
 
 UNITS = (WIDTH // 16) * (WIDTH // 128)
 HALF = UNITS // 2
@@ -46,7 +50,7 @@
 
 def kernel(
     image_ref, text_ref, head_ref, ids_ref, weight_ref,
-    loss_ref, gi_ref, gt_ref, gh_ref,
+    loss_ref, gi, gt, gh,
     image, text, head, zi, zi_inv, zt32, zt_inv, zt, zt_near, zt_far, text_far,
     ids_near, ids_far, dzt, dzi, part_near, got_near, part_far, got_far, du, du_far,
     dlog_own, dlog_near, dlog_far, loss_row, head_acc,
@@ -140,7 +144,7 @@
 
     own_ids = ids_ref[...]
     ids_image = jnp.concatenate([own_ids[i : i + 1, :] for i in range(CHUNKS)], axis=1)
-    weight = weight_ref[...].astype(F32)
+    weight = weight_ref[...].astype(F32).reshape(1, ROWS)
     loss_row[...] = jnp.zeros_like(loss_row)
 
     def tile(texts, ids_row):
@@ -210,7 +214,12 @@
     send_ids_far.wait_recv()
 
     def back(i):
-        return remote(part_far.at[rows_of(i)], got_far.at[rows_of(i)], r_send.at[i], r_recv.at[i], far)
+        rows = rows_of(i, BACK)
+        return remote(part_far.at[rows], got_far.at[rows], r_send.at[i], r_recv.at[i], far)
+
+    def send_back(first, last):
+        for j in range(first, last):
+            back(j).start()
 
     def far_tile(i):
         rows = rows_of(i)
@@ -225,6 +234,14 @@
         g = part.astype(F32)
         du_far[rows, :] = ((g - unit * jnp.sum(unit * g, axis=1, keepdims=True)) * inv).astype(BF16)
 
+    early = pl.ds(0, ROWS - CHUNK)
+    late = pl.ds(ROWS - CHUNK, CHUNK)
+
+    def head_early(i, carry):
+        cols = rows_of(i)
+        head_acc[cols, :] += dot_tn(text_far[early, cols], du_far[early, :])
+        return carry
+
     def far_step(i, carry):
         forward(i).wait_recv()
 
@@ -232,29 +249,34 @@
         def _():
             pl.semaphore_signal(gate_sem, inc=1, device_id=(z_peer(6),), device_id_type=MESH)
             pl.semaphore_wait(gate_sem, 1)
-            for j in range(CHUNKS - 1):
-                back(j).start()
+            send_back(0, BACK_1)
 
         far_tile(i)
+
+        @pl.when(i == CHUNKS - 2)
+        def _():
+            lax.fori_loop(0, WIDTH // 128, head_early, 0)
+
         return carry
 
     lax.fori_loop(0, CHUNKS, far_step, 0)
-    back(CHUNKS - 1).start()
 
     def head_all(i, carry):
+        i = (i + 4 * (1 - core)) % 9
         cols = rows_of(i)
-        total = head_acc[cols, :] + dot_tn(text_far[:, cols], du_far[...])
+        total = head_acc[cols, :] + dot_tn(text_far[late, cols], du_far[late, :])
         out = total.astype(BF16)
         for r in range(8):
             for c in range(9):
                 units[i * 72 + (r * 9 + c)] = out[16 * r : 16 * r + 16, 128 * c : 128 * c + 128]
         return carry
 
-    lax.fori_loop(0, WIDTH // 128, head_all, 0)
-    loss_core[core] = jnp.broadcast_to(jnp.sum(weight * loss_row[...]).reshape(1, 1), (8, 128))
-
+    lax.fori_loop(0, 5, head_all, 0)
     copy_a = remote(units.at[pl.ds((1 - core) * HALF, HALF)], got_a, a_send, a_recv, near)
     copy_a.start()
+    lax.fori_loop(5, 9, head_all, 0)
+    loss_core[core] = jnp.broadcast_to(jnp.sum(weight * loss_row[...]).reshape(1, 1), (8, 128))
+
     loss_a = remote(loss_core.at[core], loss_core.at[core], l_send.at[0], l_recv.at[0], near)
     loss_a.start()
 
@@ -263,16 +285,17 @@
         g = SCALE * (dzi[rows, :] + dot_tn(dlog_far[:, rows], zt_far[...]))
         inv = zi_inv[rows, :]
         unit = image[rows, :].astype(F32) * inv
-        gi_ref[rows, :] = ((g - unit * jnp.sum(unit * g, axis=1, keepdims=True)) * inv).astype(BF16)
+        gi[rows, :] = ((g - unit * jnp.sum(unit * g, axis=1, keepdims=True)) * inv).astype(BF16)
         return carry
 
     def finish_text(i):
-        back(i).wait_recv()
+        for j in range(i * CHUNK // BACK, (i + 1) * CHUNK // BACK):
+            back(j).wait_recv()
         rows = rows_of(i)
         g = dzt[rows, :] + got_far[rows, :].astype(F32)
         unit = zt32[rows, :]
         d = ((g - unit * jnp.sum(unit * g, axis=1, keepdims=True)) * zt_inv[rows, :]).astype(BF16)
-        gt_ref[rows, :] = dot_nt(d, head[...]).astype(BF16)
+        gt[rows, :] = dot_nt(d, head[...]).astype(BF16)
 
     copy_a.wait_recv()
     loss_a.wait_recv()
@@ -289,42 +312,42 @@
     first = [(x_peer, x), (y_peer, y)]
     second = [(y_peer, y), (x_peer, x)]
     copies_b = []
-    for s in range(2):
-        peer, at_s = first[s]
-        for d in (1, 2, 3):
-            to = (at_s + d) % 4
-            k = 3 * s + d - 1
-            copies_b.append(remote(half_b.at[pl.ds(STREAM * s + PIECE1 * to, PIECE1)], got_b.at[k], b_send.at[k], b_recv.at[k], peer(d)))
+    for e in (1, 2, 3, 0):
+        for s in range(2):
+            peer, at_s = first[s]
+            part = (second[s][1] + e) % 4
+            for d in (1, 2, 3):
+                to = (at_s + d) % 4
+                k = 3 * s + d - 1
+                src = half_b.at[pl.ds(STREAM * s + PIECE1 * to + PIECE2 * part, PIECE2)]
+                copies_b.append(remote(src, got_b.at[e, k], b_send.at[e, k], b_recv.at[e, k], peer(d)))
     loss_b = [remote(loss_x.at[x], loss_x.at[x], l_send.at[d], l_recv.at[d], x_peer(d)) for d in (1, 2, 3)]
     for copy in copies_b + loss_b:
         copy.start()
 
     lax.fori_loop(0, CHUNKS, finish_image, 0)
 
-    for copy in copies_b + loss_b:
+    copies_c = []
+    for n, e in enumerate((1, 2, 3, 0)):
+        for copy in copies_b[6 * n : 6 * n + 6]:
+            copy.wait_recv()
+        for s in range(2):
+            peer, at_s = second[s]
+            part = (at_s + e) % 4
+            total = half_b[pl.ds(STREAM * s + PIECE1 * first[s][1] + PIECE2 * part, PIECE2)].astype(F32)
+            for k in range(3 * s, 3 * s + 3):
+                total = total + got_b[e, k].astype(F32)
+            sum_b[s, pl.ds(PIECE2 * part, PIECE2)] = total.astype(BF16)
+            if e > 0:
+                k = 3 * s + e - 1
+                copy = remote(sum_b.at[s, pl.ds(PIECE2 * part, PIECE2)], got_c.at[k], c_send.at[k], c_recv.at[k], peer(e))
+                copy.start()
+                copies_c.append(copy)
+    for copy in loss_b:
         copy.wait_recv()
     loss_y[y] = (loss_x[0] + loss_x[1]) + (loss_x[2] + loss_x[3])
-    for s in range(2):
-        base = STREAM * s + PIECE1 * first[s][1]
-
-        def add_b(i, carry, s=s, base=base):
-            total = half_b[pl.ds(base + i * 11, 11)].astype(F32)
-            for k in range(3 * s, 3 * s + 3):
-                total = total + got_b[k, pl.ds(i * 11, 11)].astype(F32)
-            sum_b[s, pl.ds(i * 11, 11)] = total.astype(BF16)
-            return carry
-
-        lax.fori_loop(0, 4, add_b, 0)
-
-    copies_c = []
-    for s in range(2):
-        peer, at_s = second[s]
-        for d in (1, 2, 3):
-            to = (at_s + d) % 4
-            k = 3 * s + d - 1
-            copies_c.append(remote(sum_b.at[s, pl.ds(PIECE2 * to, PIECE2)], got_c.at[k], c_send.at[k], c_recv.at[k], peer(d)))
     loss_c = [remote(loss_y.at[y], loss_y.at[y], l_send.at[3 + d], l_recv.at[3 + d], y_peer(d)) for d in (1, 2, 3)]
-    for copy in copies_c + loss_c:
+    for copy in loss_c:
         copy.start()
     for copy in copies_c + loss_c:
         copy.wait_recv()
@@ -343,6 +366,7 @@
     loss_d = [remote(loss_z.at[z], loss_z.at[z], l_send.at[6 + d], l_recv.at[6 + d], z_peer(d)) for d in range(1, 8)]
     for copy in copies_d + loss_d:
         copy.start()
+    send_back(BACK_1, BACK_2)
     for copy in copies_d + loss_d:
         copy.wait_recv()
     total = sum_c[pl.ds(PIECE3 * z, PIECE3)].astype(F32)
@@ -358,8 +382,10 @@
     for copy in copies_e:
         copy.start()
     finish_text(0)
+    finish_text(1)
     for copy in copies_e:
         copy.wait_recv()
+    send_back(BACK_2, BACKS)
 
     copies_g = []
     for s in range(2):
@@ -387,7 +413,6 @@
         copy.start()
     for s in range(2):
         gat_b[s, pl.ds(PIECE1 * first[s][1], PIECE1)] = gat_c[s]
-    finish_text(1)
     for copy in copies_h:
         copy.wait_recv()
 
@@ -400,7 +425,7 @@
             def body(r, carry, s=s):
                 row = pl.ds(pl.multiple_of(which * (HALF // 9 * 16) + s * (STREAM // 9 * 16) + r * 16, 16), 16)
                 for c in range(9):
-                    gh_ref[row, 128 * c : 128 * c + 128] = src[s, r * 9 + c]
+                    gh[row, 128 * c : 128 * c + 128] = src[s, r * 9 + c]
                 return carry
 
             lax.fori_loop(0, STREAM // 9, body, 0)
@@ -417,6 +442,7 @@
     for i in range(CHUNKS):
         forward(i).wait_send()
         near_part(i).wait_send()
+    for i in range(BACKS):
         back(i).wait_send()
     for copy in [send_zt, copy_a, loss_a, copy_i] + copies_b + loss_b + copies_c + loss_c + copies_d + loss_d + copies_e + copies_g + copies_h:
         copy.wait_send()
@@ -458,7 +484,7 @@
         pltpu.VMEM((UNITS,) + unit, BF16),
         pltpu.VMEM((HALF,) + unit, BF16),
         pltpu.VMEM((HALF + 16,) + unit, BF16),
-        pltpu.VMEM((6, PIECE1) + unit, BF16),
+        pltpu.VMEM((4, 6, PIECE2) + unit, BF16),
         pltpu.VMEM((2, PIECE1) + unit, BF16),
         pltpu.VMEM((6, PIECE2) + unit, BF16),
         pltpu.VMEM((8 * PIECE3,) + unit, BF16),
@@ -476,9 +502,9 @@
         dma((2,)), dma((2,)),
         dma, dma,
         dma((CHUNKS,)), dma((CHUNKS,)),
-        dma((CHUNKS,)), dma((CHUNKS,)),
+        dma((BACKS,)), dma((BACKS,)),
         dma, dma,
-        dma((6,)), dma((6,)),
+        dma((4, 6)), dma((4, 6)),
         dma((6,)), dma((6,)),
         dma((7,)), dma((7,)),
         dma((7,)), dma((7,)),
@@ -488,22 +514,23 @@
         dma((14,)), dma((14,)),
         pltpu.SemaphoreType.REGULAR,
     ]
-    return pl.pallas_call(
+    outs = pl.pallas_call(
         kernel,
         out_shape=(
             jax.ShapeDtypeStruct((1,), F32),
-            jax.ShapeDtypeStruct(block, BF16),
-            jax.ShapeDtypeStruct(block, BF16),
-            jax.ShapeDtypeStruct((WIDTH, WIDTH), BF16),
+            pltpu.VMEM(block, BF16),
+            pltpu.VMEM(block, BF16),
+            pltpu.VMEM((WIDTH, WIDTH), BF16),
         ),
         in_specs=[anywhere, anywhere, anywhere, vmem, vmem],
         out_specs=(pl.BlockSpec(memory_space=pltpu.SMEM), vmem, vmem, vmem),
         scratch_shapes=scratch,
         compiler_params=pltpu.CompilerParams(
-            collective_id=0, has_side_effects=True, vmem_limit_bytes=58 * 1024 * 1024
+            collective_id=0, has_side_effects=True, vmem_limit_bytes=50 * 1024 * 1024
         ),
         name="contrast",
-    )(image_emb, text_feat, text_head, pair_ids.reshape(4, 128), row_weight.reshape(1, ROWS))
+    )(image_emb, text_feat, text_head, pair_ids.reshape(4, 128), row_weight)
+    return tuple(outs)
 
 
 def solution(mesh):

time: 160 us -> 138 us (0.86); the launches traced: 160 us -> 136 us
  Pallas kernels: 150 us -> 130 us
  local copies, waits for them, and re-layouts: 7.66 us -> 3.53 us
    pallas_call x1, Pallas kernels: 150 us -> 130 us  [shards(): pl.pallas_call(kernel, out_shape=(jax.ShapeDtypeStruct((1,), F32), pltpu....]
    unnamed x5 -> x3, local copies, waits for them, and re-layouts: 6.4 us -> 3.53 us
where the time goes in v3:
time: 138 us; the launch traced here: 136 us
  Pallas kernels  130 us (94%)
  local copies, waits for them, and re-layouts  3.53 us (3%)
  between operations  2.33 us (2%)
    pallas_call x1, Pallas kernels, shards(): pl.pallas_call(kernel, out_shape=(jax.ShapeDtypeStruct((1,), F32), pltpu....  130 us
    unnamed x3, local copies, waits for them, and re-layouts  3.53 us

profile of v3, /device:TPU:1, one launch (start us, length us, event | category | flops | bytes accessed | tf_op | source)
XLA Modules:
  0.0 136.1 jit_solution(5153715536184592148)
XLA Ops:
  0.6 130.2 %contrast.1 = (f32[1]{0:T(128)}, bf16[512,1152]{1,0:T(8,128)(2,1)S(1)}, bf16[512,1152]{1,0:T(8,128)(2,1)S(1)}, bf16[1152,1152]{1,0:T(8,128)(2,1)S(1)}) custom-call(bf16[512,1152]{1,0:T(8,128)(2,1)} %image_ref.1, bf16[512,1152]{1,0:T(8,128)(2,1)} %text_ref.1, bf16[1152,1152]{1,0:T(8,128)(2,1)} %head_ref.1, s32[4,128]{1,0:T(4,128)} %bitcast.1, ...), custom_call_target="tpu_custom_call" | custom-call | tf_op jit(solution)/shard_map/contrast/pallas_call | solution.py:517
  130.8 1.0 copy.13
  131.9 1.0 copy.14
  132.9 1.5 %copy.15 = bf16[1152,1152]{1,0:T(8,128)(2,1)} copy(bf16[1152,1152]{1,0:T(8,128)(2,1)S(1)} %get-tuple-element.7) | data formatting | bytes 5308416

commit v4 on v3

--- a/solution.py
+++ b/solution.py
@@ -22,7 +22,7 @@
 BACK = 64
 BACKS = ROWS // BACK
 BACK_1 = 4
-BACK_2 = 5
+BACK_2 = 4
 
 UNITS = (WIDTH // 16) * (WIDTH // 128)
 HALF = UNITS // 2

time: 138 us -> 138 us (level)
  the two profiles are of different devices: /device:TPU:1 before, /device:TPU:43 now
where the time goes in v4:
time: 138 us
  Pallas kernels  132 us (96%)
  local copies, waits for them, and re-layouts  3.53 us (3%)
  between operations  2.33 us (2%)
    pallas_call x1, Pallas kernels, shards(): pl.pallas_call(kernel, out_shape=(jax.ShapeDtypeStruct((1,), F32), pltpu....  132 us
    unnamed x3, local copies, waits for them, and re-layouts  3.53 us

profile of v4, /device:TPU:43, one launch (start us, length us, event | category | flops | bytes accessed | tf_op | source)
XLA Modules:
  0.0 137.6 jit_solution(244633741377392747)
XLA Ops:
  0.6 131.8 %contrast.1 = (f32[1]{0:T(128)}, bf16[512,1152]{1,0:T(8,128)(2,1)S(1)}, bf16[512,1152]{1,0:T(8,128)(2,1)S(1)}, bf16[1152,1152]{1,0:T(8,128)(2,1)S(1)}) custom-call(bf16[512,1152]{1,0:T(8,128)(2,1)} %image_ref.1, bf16[512,1152]{1,0:T(8,128)(2,1)} %text_ref.1, bf16[1152,1152]{1,0:T(8,128)(2,1)} %head_ref.1, s32[4,128]{1,0:T(4,128)} %bitcast.1, ...), custom_call_target="tpu_custom_call" | custom-call | tf_op jit(solution)/shard_map/contrast/pallas_call | solution.py:517
  132.4 1.0 copy.13
  133.4 1.0 copy.14
  134.5 1.5 %copy.15 = bf16[1152,1152]{1,0:T(8,128)(2,1)} copy(bf16[1152,1152]{1,0:T(8,128)(2,1)S(1)} %get-tuple-element.7) | data formatting | bytes 5308416
